TPU v7x, 32 devices: a whole 2x2x4 slice. The times are simulated.
32 devices in a mesh: groups: 2 (over x), blk: 16 (over z, y, core).
Axes of the slice: x: 2, y: 2, z: 4, core: 2. Of those that a mesh axis runs over, the one named last changes fastest.
Arguments:
- records: bfloat16 [8192, 2048], P(('groups', 'blk')), parts along dimension 0, may hold values from -6 to 6
- dest: int32 [8192, 1], P(('groups', 'blk')), parts along dimension 0, may hold values from 0 to 15; in each aligned block of 256 rows (0 to 255, 256 to 511, ...) at most 32 rows name the same one
- slot: int32 [8192, 1], P(('groups', 'blk')), parts along dimension 0, may hold values from 0 to 255
- valid: int32 [8192, 1], P(('groups', 'blk')), parts along dimension 0, may hold values from 256 to 2048
- masks: int32 [2], replicated, may hold values from 1 to 15, as said below
Outputs:
- correlations: bfloat16 [2, 4096, 128, 128], P(None, ('groups', 'blk')), parts along dimension 1
There are 2 independent parts, one for each index of `groups`. A program takes and returns all parts, laid end to end along the dimension named above; an argument that names none is the same for every part. Nothing has to cross between parts.
Inputs may be any that keep to these rules, and one draw needn't show every extreme that they name: `dest`: in the rows of one device no block is named more than 32 times. `masks`: 2 distinct numbers; one of them is 15.
All inputs are finite; a program needn't handle non-finite values.
Results may differ from a plain program's by a relative error of at most 0.0085.
Values may be sent and summed in bfloat16 or wider, within the bound.
A program may use at most 128 MiB of HBM per device.

v0:
```python
import functools
import math

import jax
import jax.numpy as jnp
import numpy as np
from jax import lax
from jax.experimental import pallas as pl
from jax.experimental.pallas import tpu as pltpu
from jax.sharding import PartitionSpec as P

CH = 128
F = 256
LAGS = 128
W = 2
EXTRA = 128
VMEM = pl.BlockSpec(memory_space=pltpu.VMEM)


def forward_table(nfft, bins):
    sample = np.arange(nfft, dtype=np.int64)[:, None]
    freq = np.arange(1, bins + 1, dtype=np.int64)[None, :]
    angle = (sample * freq % nfft).astype(np.float32) * np.float32(2.0 * math.pi / nfft)
    return np.concatenate([np.cos(angle), -np.sin(angle)], axis=1).astype(jnp.bfloat16)


def lag_table(nfft, bins, lags):
    shift = (np.arange(lags, dtype=np.int64) - lags // 2) % nfft
    freq = np.arange(1, bins + 1, dtype=np.int64)[None, :]
    angle = (freq * shift[:, None] % nfft).astype(np.float32) * np.float32(2.0 * math.pi / nfft)
    return np.concatenate([np.cos(angle), -np.sin(angle)], axis=1).astype(jnp.bfloat16)


def deliver_kernel(
    records_ref, dest_ref, slot_ref, valid_ref, table_hbm,
    tile_ref, far_ref,
    outgoing, arrived, summed, coverage, table, send_sem, recv_sem, own_sem, table_sem, far_sems,
):
    owners, capacity, wide = outgoing.shape
    held, nfft = records_ref.shape
    me = lax.axis_index("blk")

    def met(distance):
        other = me
        for k in range(owners.bit_length() - 1):
            if distance >> k & 1:
                other = other + (1 << k) * (1 - 2 * lax.rem(lax.div(me, 1 << k), 2))
        return other

    barrier = pltpu.get_barrier_semaphore()
    for distance in range(1, owners):
        pl.semaphore_signal(
            barrier, inc=1, device_id={"blk": met(distance)}, device_id_type=pl.DeviceIdType.MESH
        )
    fetch = pltpu.make_async_copy(table_hbm, table, table_sem)
    fetch.start()

    dest, slot, valid = dest_ref[...], slot_ref[...], valid_ref[...]
    onehot = (lax.broadcasted_iota(jnp.int32, (128, held), 0) == dest).astype(jnp.float32)
    before = lax.broadcasted_iota(jnp.int32, (held, held), 0) < lax.broadcasted_iota(
        jnp.int32, (held, held), 1
    )
    earlier = jnp.dot(
        onehot.astype(jnp.bfloat16),
        before.astype(jnp.float32).astype(jnp.bfloat16),
        preferred_element_type=jnp.float32,
    )
    rank = jnp.sum(earlier * onehot, axis=0, keepdims=True).astype(jnp.int32)
    position = dest * capacity + rank
    spots = owners * capacity
    place = lax.broadcasted_iota(jnp.int32, (spots, held), 0) == position
    place = place.astype(jnp.float32).astype(jnp.bfloat16)
    line = lax.broadcasted_iota(jnp.int32, (EXTRA, held), 0)
    labels = jnp.where(line == 0, slot, jnp.where(line == 1, valid >> 3, valid & 7))
    labels = labels.astype(jnp.float32).T.astype(jnp.bfloat16)
    packed = jnp.dot(place, records_ref[...], preferred_element_type=jnp.float32)
    outgoing[:, :, :nfft] = packed.astype(jnp.bfloat16).reshape(owners, capacity, nfft)
    packed = jnp.dot(place, labels, preferred_element_type=jnp.float32)
    outgoing[:, :, nfft:] = packed.astype(jnp.bfloat16).reshape(owners, capacity, EXTRA)

    pl.semaphore_wait(barrier, owners - 1)
    copies = {}
    for distance in range(owners - 1, 0, -1):
        copies[distance] = pltpu.make_async_remote_copy(
            src_ref=outgoing.at[met(distance)],
            dst_ref=arrived.at[me],
            send_sem=send_sem.at[distance],
            recv_sem=recv_sem.at[distance],
            device_id={"blk": met(distance)},
            device_id_type=pl.DeviceIdType.MESH,
        )
        copies[distance].start()
    own = pltpu.make_async_copy(outgoing.at[me], arrived.at[me], own_sem)
    own.start()

    half = owners // 2
    rows = CH * W

    def stack(base):
        block = arrived[pl.ds(base, half)].reshape(half * capacity, wide)
        marks = block[:, nfft:].astype(jnp.float32)
        reach = (marks[:, 1:2] * 8.0 + marks[:, 2:3]).astype(jnp.int32)
        goal = marks.T[0:1, :].astype(jnp.int32)
        goal = (goal & (W - 1)) * CH + lax.div(goal, W)
        select = lax.broadcasted_iota(jnp.int32, (rows, half * capacity), 0) == goal
        select = select.astype(jnp.float32).astype(jnp.bfloat16)
        window = lax.broadcasted_iota(jnp.int32, (half * capacity, nfft), 1) < reach
        window = window.astype(jnp.float32).astype(jnp.bfloat16)
        data = block[:, :nfft] * window
        return (
            jnp.dot(select, data, preferred_element_type=jnp.float32),
            jnp.dot(select, window, preferred_element_type=jnp.float32),
        )

    near_base = lax.div(me, half) * half
    own.wait()
    for distance in range(half - 1, 0, -1):
        copies[distance].wait_recv()
    summed[...], coverage[...] = stack(near_base)
    for distance in range(owners - 1, half - 1, -1):
        copies[distance].wait_recv()
    total, count = stack(half - near_base)
    trace = (summed[...] + total) / jnp.maximum(coverage[...] + count, 1.0)
    meansq = jnp.mean(trace * trace, axis=1, keepdims=True)
    normed = (trace * lax.rsqrt(meansq + 1e-06)).astype(jnp.bfloat16)
    fetch.wait()
    spectrum = jnp.dot(normed, table[...], preferred_element_type=jnp.float32)
    real_part, imag_part = spectrum[:, :F], spectrum[:, F:]
    amplitude = lax.rsqrt(jnp.maximum(real_part * real_part + imag_part * imag_part, nfft / 4.0))
    real_part = (real_part * amplitude).astype(jnp.bfloat16)
    imag_part = (imag_part * amplitude).astype(jnp.bfloat16)
    for w in range(W):
        base = 2 * F * w
        tile_ref[:, base : base + F] = real_part[w * CH : (w + 1) * CH]
        tile_ref[:, base + F : base + 2 * F] = imag_part[w * CH : (w + 1) * CH]
    across = pltpu.make_async_remote_copy(
        src_ref=tile_ref,
        dst_ref=far_ref,
        send_sem=far_sems.at[0],
        recv_sem=far_sems.at[1],
        device_id={"blk": met(owners - 1)},
        device_id_type=pl.DeviceIdType.MESH,
    )
    across.start()
    for distance in range(owners - 1, 0, -1):
        copies[distance].wait_send()
    across.wait()


def correlate_kernel(far_round_ref, own_ref, other_ref, table_ref, out_ref, turned):
    scale = 1.0 / math.sqrt(W * F)
    cosine, sine = table_ref[:, :F], table_ref[:, F:]
    far_round = far_round_ref[0]
    slots, step = turned.shape[0], own_ref.shape[1]

    for index in range(step // 2):
        at = index % slots
        for half in range(2):
            mine = own_ref[0, index * 2 + half : index * 2 + half + 1, :].astype(jnp.bfloat16)
            rows = slice(half * LAGS, (half + 1) * LAGS)
            for w in range(W):
                base = 2 * F * w
                ur, ui = mine[:, base : base + F], mine[:, base + F : base + 2 * F]
                turned[at, rows, base : base + F] = cosine * ur + sine * ui
                turned[at, rows, base + F : base + 2 * F] = cosine * ui - sine * ur
        product = lax.dot_general(
            other_ref[...],
            turned[at],
            (((1,), (1,)), ((), ())),
            preferred_element_type=jnp.float32,
        )
        product = (product * scale).astype(jnp.bfloat16)
        for half in range(2):
            lags = slice(half * LAGS, (half + 1) * LAGS)
            out_ref[far_round, index * 2 + half] = product[:CH, lags]
            out_ref[1 - far_round, index * 2 + half] = product[CH:, lags]


def local(records, dest, slot, valid, masks):
    owners = lax.axis_size("blk")
    held, nfft = records.shape
    rounds = masks.shape[0]
    capacity = max(16, 2 * held // owners)
    width = 2 * F * W
    big = pltpu.CompilerParams(vmem_limit_bytes=56 * 2**20)
    slots = pltpu.VMEM((owners, capacity, nfft + EXTRA), jnp.bfloat16)
    tile, far = pl.pallas_call(
        deliver_kernel,
        out_shape=[jax.ShapeDtypeStruct((CH, width), jnp.bfloat16)] * 2,
        in_specs=[VMEM] * 4 + [pl.BlockSpec(memory_space=pl.ANY)],
        out_specs=[VMEM] * 2,
        scratch_shapes=[
            slots,
            slots,
            pltpu.VMEM((CH * W, nfft), jnp.float32),
            pltpu.VMEM((CH * W, nfft), jnp.float32),
            pltpu.VMEM((nfft, 2 * F), jnp.bfloat16),
            pltpu.SemaphoreType.DMA((owners,)),
            pltpu.SemaphoreType.DMA((owners,)),
            pltpu.SemaphoreType.DMA,
            pltpu.SemaphoreType.DMA,
            pltpu.SemaphoreType.DMA((2,)),
        ],
        compiler_params=pltpu.CompilerParams(
            vmem_limit_bytes=56 * 2**20, collective_id=0, has_side_effects=True
        ),
        name="deliver",
    )(
        records,
        dest.reshape(1, held),
        slot.reshape(1, held),
        valid.reshape(1, held),
        jnp.asarray(forward_table(nfft, F)),
    )
    last = owners - 1
    top = 1 << (owners.bit_length() - 2)

    def swap(block, distance):
        return lax.ppermute(block, "blk", [(b, b ^ distance) for b in range(owners)])

    def branch(mask):
        if mask & top:
            return lambda mine, met: swap(met, last ^ mask)
        return lambda mine, met: swap(mine, mask)

    second = masks[0] ^ masks[1] ^ last
    near = lax.switch(second - 1, [branch(m) for m in range(1, last)], tile, far)
    far_round = jnp.where(masks[0] == last, 0, 1).astype(jnp.int32).reshape(1)
    other = jnp.concatenate([far, near], axis=0)
    step = 16
    return pl.pallas_call(
        correlate_kernel,
        grid=(CH // step,),
        out_shape=jax.ShapeDtypeStruct((rounds, CH, CH, LAGS), jnp.bfloat16),
        in_specs=[
            pl.BlockSpec(memory_space=pltpu.SMEM),
            pl.BlockSpec((1, step, width), lambda i: (i, 0, 0)),
            pl.BlockSpec((rounds * CH, width), lambda i: (0, 0)),
            pl.BlockSpec((LAGS, 2 * F), lambda i: (0, 0)),
        ],
        out_specs=pl.BlockSpec((rounds, step, CH, LAGS), lambda i: (0, i, 0, 0)),
        scratch_shapes=[pltpu.VMEM((4, 2 * LAGS, width), jnp.bfloat16)],
        compiler_params=big,
        name="correlate",
    )(
        far_round,
        tile.astype(jnp.float32).reshape(CH // step, step, width),
        other,
        jnp.asarray(lag_table(nfft, F, LAGS)),
    )


def solution(mesh):
    return jax.shard_map(
        local,
        mesh=mesh,
        in_specs=(
            P(("groups", "blk"), None),
            P(("groups", "blk"), None),
            P(("groups", "blk"), None),
            P(("groups", "blk"), None),
            P(),
        ),
        out_specs=P(None, ("groups", "blk"), None, None),
        check_vma=False,
    )
```

profile of v0, /device:TPU:1, one launch (start us, length us, event | category | flops | bytes accessed | tf_op | source)
XLA Modules:
  0.0 97.1 jit_solution(3469279863031551693)
XLA Ops:
  0.0 1.3 %fusion = (s32[1]{0:T(128)}, s32[1]{0:T(128)}) fusion(s32[2]{0:T(128)} %param.25), kind=kLoop, calls=%fused_computation.1 | loop fusion | bytes 16 | tf_op jit(solution)/shard_map/slice | solution.py:226
  3.2 70.5 %deliver.1 = (bf16[128,1024]{1,0:T(8,128)(2,1)S(1)}, bf16[128,1024]{1,0:T(8,128)(2,1)S(1)}) custom-call(bf16[256,2048]{1,0:T(8,128)(2,1)} %records_ref.1, s32[1,256]{1,0:T(1,128)} %bitcast.7, s32[1,256]{1,0:T(1,128)} %bitcast.8, s32[1,256]{1,0:T(1,128)} %bitcast.9, bf16[2048,512]{1,0:T(8,128)(2,1)} %constant.21.clone.table_hbm), custom_call_target="tpu_custom_call" | custom-call | tf_op jit(solution)/shard_map/deliver/pallas_call | solution.py:187
  73.8 7.8 %conditional.1 = (bf16[128,1024]{1,0:T(8,128)(2,1)}) conditional(s32[]{:T(128)} %bitcast.4, bf16[128,1024]{1,0:T(8,128)(2,1)S(1)} %get-tuple-element.36, bf16[128,1024]{1,0:T(8,128)(2,1)S(1)} %get-tuple-element.36, bf16[128,1024]{1,0:T(8,128)(2,1)S(1)} %get-tuple-element.36, ...), branch_computations={%region_0.0_spmd, %region_1.0_spmd, %region_2.0_spmd, %region_3.0_... | conditional | bytes 1048624 | solution.py:227
  73.8 1.2 %collective-permute-start.12 = (bf16[128,1024]{1,0:T(8,128)(2,1)S(1)}, bf16[128,1024]{1,0:T(8,128)(2,1)}, u32[]{:S(2)}, u32[]{:S(2)}) collective-permute-start(bf16[128,1024]{1,0:T(8,128)(2,1)S(1)} %param.12), channel_id=1, source_target_pairs={{0,2},{1,3},{2,0},{3,1},{4,6},{5,7},{6,4},{7,5},{8,10},{9,11},{10,... | collective-permute-start | bytes 786440 | tf_op jit(solution)/shard_map/cond/branch_12_fun/ppermute | solution.py:219
  75.1 6.5 %collective-permute-done.12 = bf16[128,1024]{1,0:T(8,128)(2,1)} collective-permute-done((bf16[128,1024]{1,0:T(8,128)(2,1)S(1)}, bf16[128,1024]{1,0:T(8,128)(2,1)}, u32[]{:S(2)}, u32[]{:S(2)}) %collective-permute-start.12) | collective-permute-done | bytes 262176 | tf_op jit(solution)/shard_map/cond/branch_12_fun/ppermute | solution.py:219
  81.6 1.8 %pad_maximum_fusion.other_ref = bf16[256,1024]{1,0:T(8,128)(2,1)} fusion(bf16[128,1024]{1,0:T(8,128)(2,1)} %get-tuple-element.40, bf16[128,1024]{1,0:T(8,128)(2,1)S(1)} %get-tuple-element.37), kind=kLoop, calls=%fused_computation | loop fusion | flops 1048576 | bytes 1048576 | tf_op jit(solution)/shard_map/concatenate | solution.py:229
  83.4 0.9 convert.1.own_ref
  84.2 12.9 %correlate.1 = bf16[2,128,128,128]{3,2,1,0:T(8,128)(2,1)} custom-call(s32[1]{0:T(128)S(6)} %select_n.5.far_round_ref, f32[8,16,1024]{2,1,0:T(8,128)} %convert.1.own_ref, bf16[256,1024]{1,0:T(8,128)(2,1)} %pad_maximum_fusion.other_ref, bf16[128,512]{1,0:T(8,128)(2,1)} %constant.22.clone.table_ref), custom_call_target="tpu_custom_call" | custom-call | tf_op jit(solution)/shard_map/correlate/pallas_call | solution.py:231
Async XLA Ops:
  73.8 7.8 %collective-permute-start.12 = (bf16[128,1024]{1,0:T(8,128)(2,1)S(1)}, bf16[128,1024]{1,0:T(8,128)(2,1)}, u32[]{:S(2)}, u32[]{:S(2)}) collective-permute-start(bf16[128,1024]{1,0:T(8,128)(2,1)S(1)} %param.12), channel_id=1, source_target_pairs={{0,2},{1,3},{2,0},{3,1},{4,6},{5,7},{6,4},{7,5},{8,10},{9,11},{10,... | collective-permute-start | bytes 786440 | tf_op jit(solution)/shard_map/cond/branch_12_fun/ppermute | solution.py:219
where the time goes:
time: 98.3 us; the launch traced here: 97.1 us
  Pallas kernels  83.4 us (85%)
  waiting for transfers between devices  6.55 us (7%)
  other arithmetic  2.63 us (3%)
  between operations  1.94 us (2%)
  local copies, waits for them, and re-layouts  1.31 us (1%)
  starting transfers between devices  1.25 us (1%)
    pallas_call x1, Pallas kernels, local(): pl.pallas_call(deliver_kernel, out_shape=[jax.ShapeDtypeStruct((CH, width...  70.5 us
    pallas_call x1, Pallas kernels, local(): pl.pallas_call(correlate_kernel, grid=(CH // step,), out_shape=jax.ShapeD...  12.9 us
    ppermute x1, waiting for transfers between devices, swap(): lax.ppermute(block, 'blk', [(b, b ^ distance) for b in range(owners)])  6.55 us
  transfers between devices with their start and end apart: 1, of which 1 were waited for; matrix products, arithmetic and copies ran while one was open for 0% of the time, Pallas kernels for 0%

commit v1 on v0

v1 whole, which is shorter than its diff:
```python
import functools
import math

import jax
import jax.numpy as jnp
import numpy as np
from jax import lax
from jax.experimental import pallas as pl
from jax.experimental.pallas import tpu as pltpu
from jax.sharding import PartitionSpec as P

CH = 128
F = 256
LAGS = 128
W = 2
GROUP = 4
CHUNK = 256
PIECES = 4
GAP = 64.0
LEVELS = ((96, 96, 96, 80, 64, 64, 48, 32), (112, 112, 112, 96, 80, 64, 48, 32))
VMEM = pl.BlockSpec(memory_space=pltpu.VMEM)
SMEM = pl.BlockSpec(memory_space=pltpu.SMEM)
MESH = pl.DeviceIdType.MESH


def forward_table(nfft, bins):
    sample = np.arange(nfft, dtype=np.int64)[:, None]
    freq = np.arange(1, bins + 1, dtype=np.int64)[None, :]
    angle = (sample * freq % nfft).astype(np.float32) * np.float32(2.0 * math.pi / nfft)
    return np.concatenate([np.cos(angle), -np.sin(angle)], axis=1).astype(jnp.bfloat16)


def lag_table(nfft, bins, lags):
    shift = (np.arange(lags, dtype=np.int64) - lags // 2) % nfft
    freq = np.arange(1, bins + 1, dtype=np.int64)[None, :]
    angle = (freq * shift[:, None] % nfft).astype(np.float32) * np.float32(2.0 * math.pi / nfft)
    return np.concatenate([np.cos(angle), -np.sin(angle)], axis=1).astype(jnp.bfloat16)


def met_at(me, distance, owners):
    other = me
    for k in range(owners.bit_length() - 1):
        if distance >> k & 1:
            other = other + (1 << k) * (1 - 2 * lax.rem(lax.div(me, 1 << k), 2))
    return other


def gathered_at(distance):
    bits = GROUP.bit_length() - 1
    return sum((distance >> k & 1) << (bits - 1 - k) for k in range(bits))


def capacities(most, chunks):
    found = []
    for level in LEVELS:
        rows = [-(-level[c * len(level) // chunks] * most // (128 * 16)) * 16 for c in range(chunks)]
        rows = tuple(min(most, max(16, r)) for r in rows)
        if rows not in found:
            found.append(rows)
    full = (most,) * chunks
    return [rows for rows in found if rows != full] + [full]


def plan_kernel(
    records_ref, dest_ref, slot_ref, valid_ref,
    outgoing_ref, goal_ref, level_ref,
    outbox, inbox, levels, send_sem, recv_sem, level_sems,
):
    chunks, planes, most, wide = outgoing_ref.shape
    owners = planes * GROUP
    held = records_ref.shape[0]
    me, part = lax.axis_index("blk"), lax.axis_index("groups")
    parts = levels.shape[0]
    plane = lax.div(me, GROUP)

    barrier = pltpu.get_barrier_semaphore()
    for distance in range(1, owners):
        pl.semaphore_signal(
            barrier, inc=1, device_id={"blk": met_at(me, distance, owners)}, device_id_type=MESH
        )
    for distance in range(1, parts):
        pl.semaphore_signal(
            barrier, inc=1, device_id={"groups": lax.rem(part + distance, parts)}, device_id_type=MESH
        )

    dest, slot, valid = dest_ref[...], slot_ref[...], valid_ref[...]
    group, within = lax.div(dest, GROUP), lax.rem(dest, GROUP)
    key = valid * held + (held - 1 - lax.broadcasted_iota(jnp.int32, (1, held), 1))
    line = lax.broadcasted_iota(jnp.int32, (8, held), 0)
    columns = jnp.where(line == 0, group, jnp.where(line == 1, key, valid)).astype(jnp.float32).T
    key, group_row = key.astype(jnp.float32), group.astype(jnp.float32)
    ahead = (columns[:, 1:2] > key) & (columns[:, 0:1] == group_row)
    rank = jnp.sum(ahead.astype(jnp.float32), axis=0, keepdims=True).astype(jnp.int32)
    reach = lax.div(valid - 1, wide)
    level = jnp.zeros((1, held), jnp.float32)
    for rows in capacities(most, chunks)[:-1]:
        limit = jnp.zeros((1, held), jnp.int32)
        for c in range(chunks):
            limit = jnp.where(reach == c, rows[c], limit)
        level = level + jnp.max((rank >= limit).astype(jnp.float32), axis=1, keepdims=True)
    levels[0] = level[:, :128]

    pl.semaphore_wait(barrier, owners - 1 + parts - 1)
    sideways = []
    for distance in range(1, parts):
        sideways.append(
            pltpu.make_async_remote_copy(
                src_ref=levels.at[0],
                dst_ref=levels.at[distance],
                send_sem=level_sems.at[0, distance],
                recv_sem=level_sems.at[1, distance],
                device_id={"groups": lax.rem(part + distance, parts)},
                device_id_type=MESH,
            )
        )
        sideways[-1].start()

    lines = max(8, planes)
    named = lax.broadcasted_iota(jnp.int32, (lines, held), 0) == group
    ranked = (lax.broadcasted_iota(jnp.int32, (128, held), 0) == rank).astype(jnp.float32)
    ranked = ranked.astype(jnp.bfloat16)

    def spread(values):
        values = jnp.where(named, values, 0).astype(jnp.float32).astype(jnp.bfloat16)
        return lax.dot_general(
            values, ranked, (((1,), (1,)), ((), ())), preferred_element_type=jnp.float32
        )

    code = spread(within + 1) * 256.0 + spread(slot)
    for p in range(planes):
        outbox[p, 0:1, :] = code[p : p + 1]

    for copy in sideways:
        copy.wait()
    level = levels[0]
    for distance in range(1, parts):
        level = jnp.maximum(level, levels[distance])
    for p in range(planes):
        outbox[p, 1:2, :] = level
    copies = []
    for distance in range(owners - 1, 0, -1):
        other = met_at(me, distance, owners)
        copies.append(
            pltpu.make_async_remote_copy(
                src_ref=outbox.at[lax.div(other, GROUP)],
                dst_ref=inbox.at[gathered_at(distance % GROUP) * planes + plane],
                send_sem=send_sem.at[distance],
                recv_sem=recv_sem.at[distance],
                device_id={"blk": other},
                device_id_type=MESH,
            )
        )
        copies[-1].start()
    inbox[plane] = outbox[plane]

    spots = planes * most
    place = lax.broadcasted_iota(jnp.int32, (spots, held), 0) == group * most + rank
    place = place.astype(jnp.float32).astype(jnp.bfloat16)
    ends = columns[:, 2:3].astype(jnp.int32)
    for c in range(chunks):
        window = lax.broadcasted_iota(jnp.int32, (held, wide), 1) + c * wide < ends
        window = window.astype(jnp.float32).astype(jnp.bfloat16)
        data = records_ref[:, c * wide : (c + 1) * wide] * window + (GAP - GAP * window)
        packed = jnp.dot(place, data, preferred_element_type=jnp.float32)
        outgoing_ref[c] = packed.astype(jnp.bfloat16).reshape(planes, most, wide)

    for copy in copies:
        copy.wait()
    code = inbox[:, 0, :]
    level_ref[0] = jnp.max(inbox[:, 1, :]).astype(jnp.int32)
    kept = owners * most
    at = lax.broadcasted_iota(jnp.int32, (128, kept), 1)
    sown = lax.broadcasted_iota(jnp.int32, (128, kept), 0) == lax.rem(at, most)
    sown = sown.astype(jnp.float32).astype(jnp.bfloat16)
    owner = (code * (1.0 / 256.0)).astype(jnp.int32).astype(jnp.float32)
    slots = code - owner * 256.0
    at = lax.broadcasted_iota(jnp.int32, (owners, kept), 1)
    mine = lax.broadcasted_iota(jnp.int32, (owners, kept), 0) == lax.div(at, most)

    def line_up(values):
        values = jnp.dot(values.astype(jnp.bfloat16), sown, preferred_element_type=jnp.float32)
        return jnp.sum(jnp.where(mine, values, 0.0), axis=0, keepdims=True).astype(jnp.int32)

    slots = line_up(slots)
    goal = lax.rem(slots, W) * CH + lax.div(slots, W)
    goal_ref[...] = jnp.where(line_up(owner) == lax.rem(me, GROUP) + 1, goal, -1)


def deliver_kernel(
    caps, outgoing_ref, goal_ref, masks_ref, table_hbm,
    own_ref, met_ref,
    arrived, select, table, spectrum, energy, tile, leaving, landing,
    plane_send, plane_recv, gather_send, gather_recv, own_sem, table_sem,
    far_send, far_recv, hop_send, hop_recv,
):
    chunks, _, planes, most, wide = arrived.shape
    owners = planes * GROUP
    nfft = chunks * wide
    kept = owners * most
    me = lax.axis_index("blk")
    plane = lax.div(me, GROUP)
    last = owners - 1
    bits = list(range(owners.bit_length() - 3, -1, -1))
    steps = list(range(GROUP.bit_length() - 2, -1, -1))

    for c in range(chunks):
        if caps[c] < most:
            rest = arrived.at[c, :, :, caps[c] :, :]
            rest[...] = jnp.full(rest.shape, GAP, jnp.bfloat16)
    barrier = pltpu.get_barrier_semaphore()
    peers = {GROUP * d for d in range(1, planes)} | {1 << k for k in steps + bits} | {last}
    for distance in sorted(peers):
        pl.semaphore_signal(
            barrier, inc=1, device_id={"blk": met_at(me, distance, owners)}, device_id_type=MESH
        )
    fetch = pltpu.make_async_copy(table_hbm, table, table_sem)
    fetch.start()
    pl.semaphore_wait(barrier, len(peers))

    def send(distance, source, target, send_sem, recv_sem):
        copy = pltpu.make_async_remote_copy(
            src_ref=source,
            dst_ref=target,
            send_sem=send_sem,
            recv_sem=recv_sem,
            device_id={"blk": met_at(me, distance, owners)},
            device_id_type=MESH,
        )
        copy.start()
        return copy

    sent, local, gathers = {}, {}, {}

    def begin(c):
        rows = pl.ds(0, caps[c])
        for d in range(planes - 1, 0, -1):
            other = lax.div(met_at(me, GROUP * d, owners), GROUP)
            sent[c, d] = send(
                GROUP * d,
                outgoing_ref.at[c, other, rows],
                arrived.at[c, 0, plane, rows],
                plane_send.at[c, d],
                plane_recv.at[c, d],
            )
        local[c] = pltpu.make_async_copy(
            outgoing_ref.at[c, plane, rows], arrived.at[c, 0, plane, rows], own_sem.at[c]
        )
        local[c].start()

    def forward(c, step, part):
        low, count = (0, 1) if part == 0 else (1 << (part - 1), 1 << (part - 1))
        rows = pl.ds(0, caps[c])
        gathers[c, step, part] = send(
            1 << steps[step],
            arrived.at[c, pl.ds(low, count), :, rows],
            arrived.at[c, pl.ds(low + (1 << step), count), :, rows],
            gather_send.at[c, step, part],
            gather_recv.at[c, step, part],
        )

    goal = goal_ref[...]
    width = min(512, kept)
    for base in range(0, kept, width):
        chosen = lax.broadcasted_iota(jnp.int32, (CH * W, width), 0) == goal[:, base : base + width]
        select[:, base : base + width] = chosen.astype(jnp.float32).astype(jnp.bfloat16)

    def compute(c):
        data = arrived[c].reshape(kept, wide)
        window = jnp.minimum(jnp.maximum(GAP / 2 - data, 0.0), 1.0)
        total = jnp.dot(select[...], data * window, preferred_element_type=jnp.float32)
        count = jnp.dot(select[...], window, preferred_element_type=jnp.float32)
        trace = total / jnp.maximum(count, 1.0)
        squares = trace * trace
        squares = sum(squares[:, k : k + 128] for k in range(0, wide, 128))
        part = jnp.dot(
            trace.astype(jnp.bfloat16),
            table[c * wide : (c + 1) * wide, :],
            preferred_element_type=jnp.float32,
        )
        if c == 0:
            energy[...], spectrum[...] = squares, part
        else:
            energy[...] += squares
            spectrum[...] += part

    ahead = min(3, chunks)
    for c in range(ahead):
        begin(c)
    depth = len(steps)
    for turn in range(chunks + depth + 1):
        for stage in range(depth + 1, -1, -1):
            c = turn - stage
            if not 0 <= c < chunks:
                continue
            if stage == 0:
                for d in range(planes - 1, 0, -1):
                    sent[c, d].wait_recv()
                local[c].wait()
                if c + ahead < chunks:
                    begin(c + ahead)
                for step in range(depth):
                    forward(c, step, 0)
            elif stage <= depth:
                for part in range(stage):
                    gathers[c, stage - 1, part].wait_recv()
                for step in range(stage, depth):
                    forward(c, step, stage)
            if stage == depth:
                if c == 0:
                    fetch.wait()
                compute(c)

    second = masks_ref[0] ^ masks_ref[1] ^ last
    use_far = lax.div(second, 1 << (len(bits)))
    path = second + use_far * (last - 2 * second)
    size = CH // PIECES

    def choose(flag, yes, no):
        flag = jnp.full(yes.shape, flag.astype(jnp.float32), jnp.float32).astype(jnp.bfloat16)
        return yes * flag + no * (1 - flag)

    factor = lax.rsqrt(jnp.sum(energy[...], axis=1, keepdims=True) * (1.0 / nfft) + 1e-06)
    far = []
    for q in range(PIECES):
        rows = slice(q * size, (q + 1) * size)
        for w in range(W):
            at = slice(w * CH + q * size, w * CH + (q + 1) * size)
            parts = spectrum[at, :] * factor[at]
            real_part, imag_part = parts[:, :F], parts[:, F:]
            amplitude = lax.rsqrt(
                jnp.maximum(real_part * real_part + imag_part * imag_part, nfft / 4.0)
            )
            real_part = (real_part * amplitude).astype(jnp.bfloat16)
            imag_part = (imag_part * amplitude).astype(jnp.bfloat16)
            base = 2 * F * w
            tile[rows, base : base + F] = real_part
            tile[rows, base + F : base + 2 * F] = imag_part
            own_ref[rows, base : base + F] = real_part.astype(jnp.float32)
            own_ref[rows, base + F : base + 2 * F] = imag_part.astype(jnp.float32)
        rows = pl.ds(q * size, size)
        far.append(send(last, tile.at[rows], met_ref.at[rows], far_send.at[q], far_recv.at[q]))

    hops = {}
    for turn in range(PIECES + len(bits)):
        for stage in range(len(bits), -1, -1):
            q = turn - stage
            if not 0 <= q < PIECES:
                continue
            rows = slice(q * size, (q + 1) * size)
            if stage == 0:
                far[q].wait_recv()
                value = choose(use_far, met_ref[rows], tile[rows])
            else:
                hops[stage - 1, q].wait_recv()
                taken = lax.rem(lax.div(path, 1 << bits[stage - 1]), 2)
                value = choose(taken, landing[stage - 1, rows], leaving[stage - 1, rows])
            if stage == len(bits):
                met_ref[CH + q * size : CH + (q + 1) * size] = value
            else:
                leaving[stage, rows] = value
                spot = pl.ds(q * size, size)
                hops[stage, q] = send(
                    1 << bits[stage],
                    leaving.at[stage, spot],
                    landing.at[stage, spot],
                    hop_send.at[stage, q],
                    hop_recv.at[stage, q],
                )
    for copy in list(sent.values()) + list(gathers.values()) + far + list(hops.values()):
        copy.wait_send()


def correlate_kernel(masks_ref, own_ref, other_ref, table_ref, out_ref, turned, *, last):
    scale = 1.0 / math.sqrt(W * F)
    cosine, sine = table_ref[:, :F], table_ref[:, F:]
    far_round = (masks_ref[0] != last).astype(jnp.int32)
    slots, step = turned.shape[0], own_ref.shape[1]

    for index in range(step // 2):
        at = index % slots
        for half in range(2):
            mine = own_ref[0, index * 2 + half : index * 2 + half + 1, :].astype(jnp.bfloat16)
            rows = slice(half * LAGS, (half + 1) * LAGS)
            for w in range(W):
                base = 2 * F * w
                ur, ui = mine[:, base : base + F], mine[:, base + F : base + 2 * F]
                turned[at, rows, base : base + F] = cosine * ur + sine * ui
                turned[at, rows, base + F : base + 2 * F] = cosine * ui - sine * ur
        product = lax.dot_general(
            other_ref[...],
            turned[at],
            (((1,), (1,)), ((), ())),
            preferred_element_type=jnp.float32,
        )
        product = (product * scale).astype(jnp.bfloat16)
        for half in range(2):
            lags = slice(half * LAGS, (half + 1) * LAGS)
            out_ref[far_round, index * 2 + half] = product[:CH, lags]
            out_ref[1 - far_round, index * 2 + half] = product[CH:, lags]


def local(records, dest, slot, valid, masks):
    owners, parts = lax.axis_size("blk"), lax.axis_size("groups")
    held, nfft = records.shape
    rounds = masks.shape[0]
    planes, chunks = owners // GROUP, nfft // CHUNK
    most = max(16, GROUP * 2 * held // owners)
    width = 2 * F * W
    limit = 56 * 2**20
    outgoing, goal, level = pl.pallas_call(
        plan_kernel,
        out_shape=[
            jax.ShapeDtypeStruct((chunks, planes, most, CHUNK), jnp.bfloat16),
            jax.ShapeDtypeStruct((1, owners * most), jnp.int32),
            jax.ShapeDtypeStruct((1,), jnp.int32),
        ],
        in_specs=[VMEM] * 4,
        out_specs=[VMEM, VMEM, SMEM],
        scratch_shapes=[
            pltpu.VMEM((planes, 2, 128), jnp.float32),
            pltpu.VMEM((owners, 2, 128), jnp.float32),
            pltpu.VMEM((parts, 1, 128), jnp.float32),
            pltpu.SemaphoreType.DMA((owners,)),
            pltpu.SemaphoreType.DMA((owners,)),
            pltpu.SemaphoreType.DMA((2, parts)),
        ],
        compiler_params=pltpu.CompilerParams(
            vmem_limit_bytes=limit, collective_id=0, has_side_effects=True
        ),
        name="plan",
    )(records, dest.reshape(1, held), slot.reshape(1, held), valid.reshape(1, held))

    last = owners - 1
    hops = owners.bit_length() - 2
    depth = GROUP.bit_length() - 1

    def deliver(number, caps):
        def call(outgoing, goal, masks, table):
            return pl.pallas_call(
                functools.partial(deliver_kernel, caps),
                out_shape=[
                    jax.ShapeDtypeStruct((CH, width), jnp.float32),
                    jax.ShapeDtypeStruct((rounds * CH, width), jnp.bfloat16),
                ],
                in_specs=[pl.BlockSpec(memory_space=pl.ANY), VMEM, SMEM, pl.BlockSpec(memory_space=pl.ANY)],
                out_specs=[VMEM] * 2,
                scratch_shapes=[
                    pltpu.VMEM((chunks, GROUP, planes, most, CHUNK), jnp.bfloat16),
                    pltpu.VMEM((CH * W, owners * most), jnp.bfloat16),
                    pltpu.VMEM((nfft, 2 * F), jnp.bfloat16),
                    pltpu.VMEM((CH * W, 2 * F), jnp.float32),
                    pltpu.VMEM((CH * W, 128), jnp.float32),
                    pltpu.VMEM((CH, width), jnp.bfloat16),
                    pltpu.VMEM((hops, CH, width), jnp.bfloat16),
                    pltpu.VMEM((hops, CH, width), jnp.bfloat16),
                    pltpu.SemaphoreType.DMA((chunks, planes)),
                    pltpu.SemaphoreType.DMA((chunks, planes)),
                    pltpu.SemaphoreType.DMA((chunks, depth, depth)),
                    pltpu.SemaphoreType.DMA((chunks, depth, depth)),
                    pltpu.SemaphoreType.DMA((chunks,)),
                    pltpu.SemaphoreType.DMA,
                    pltpu.SemaphoreType.DMA((PIECES,)),
                    pltpu.SemaphoreType.DMA((PIECES,)),
                    pltpu.SemaphoreType.DMA((hops, PIECES)),
                    pltpu.SemaphoreType.DMA((hops, PIECES)),
                ],
                compiler_params=pltpu.CompilerParams(
                    vmem_limit_bytes=limit, collective_id=number, has_side_effects=True
                ),
                name=f"deliver{number}",
            )(outgoing, goal, masks, table)

        return call

    sizes = capacities(most, chunks)
    calls = [deliver(number + 1, caps) for number, caps in enumerate(sizes)]
    own, other = lax.switch(
        level[0], calls, outgoing, goal, masks, jnp.asarray(forward_table(nfft, F))
    )
    step = 16
    return pl.pallas_call(
        functools.partial(correlate_kernel, last=last),
        grid=(CH // step,),
        out_shape=jax.ShapeDtypeStruct((rounds, CH, CH, LAGS), jnp.bfloat16),
        in_specs=[
            SMEM,
            pl.BlockSpec((1, step, width), lambda i: (i, 0, 0)),
            pl.BlockSpec((rounds * CH, width), lambda i: (0, 0)),
            pl.BlockSpec((LAGS, 2 * F), lambda i: (0, 0)),
        ],
        out_specs=pl.BlockSpec((rounds, step, CH, LAGS), lambda i: (0, i, 0, 0)),
        scratch_shapes=[pltpu.VMEM((4, 2 * LAGS, width), jnp.bfloat16)],
        compiler_params=pltpu.CompilerParams(vmem_limit_bytes=limit),
        name="correlate",
    )(
        masks,
        own.reshape(CH // step, step, width),
        other,
        jnp.asarray(lag_table(nfft, F, LAGS)),
    )


def solution(mesh):
    return jax.shard_map(
        local,
        mesh=mesh,
        in_specs=(
            P(("groups", "blk"), None),
            P(("groups", "blk"), None),
            P(("groups", "blk"), None),
            P(("groups", "blk"), None),
            P(),
        ),
        out_specs=P(None, ("groups", "blk"), None, None),
        check_vma=False,
    )
```

time: 98.3 us -> 104 us (1.058); the launches traced: 97.1 us -> 104 us
  Pallas kernels: 83.4 us -> 103 us
  waiting for transfers between devices: 6.55 us -> 0 us
  other arithmetic: 2.63 us -> 0 us
  between operations: 1.94 us -> 0.58 us
  local copies, waits for them, and re-layouts: 1.31 us -> 0 us
  starting transfers between devices: 1.25 us -> 0 us
    pallas_call x2 -> x3, Pallas kernels: 83.4 us -> 103 us  [the longest x1 77.5 us: call(): pl.pallas_call(functools.partial(deliver_kernel, caps), out_shape=[jax.Sh...]
    ppermute x1 -> x0, waiting for transfers between devices: 6.55 us -> none  [swap(): lax.ppermute(block, 'blk', [(b, b ^ distance) for b in range(owners)])]
    concatenate x1 -> x0, other arithmetic: 1.78 us -> none  [local(): other = jnp.concatenate([far, near], axis=0)]
    slice x1 -> x0, local copies, waits for them, and re-layouts: 1.31 us -> none  [local(): second = masks[0] ^ masks[1] ^ last]
    ppermute x1 -> x0, starting transfers between devices: 1.25 us -> none  [swap(): lax.ppermute(block, 'blk', [(b, b ^ distance) for b in range(owners)])]
  transfers between devices with their start and end apart: 1 -> 0, of which waited for: 1 -> 0; matrix products, arithmetic and copies ran while one was open for 0% -> 0% of each run, Pallas kernels for 0% -> 0%
where the time goes in v1:
time: 104 us
  Pallas kernels  103 us (99%)
    pallas_call x1, Pallas kernels, call(): pl.pallas_call(functools.partial(deliver_kernel, caps), out_shape=[jax.Sh...  77.5 us
    pallas_call x1, Pallas kernels, local(): pl.pallas_call(plan_kernel, out_shape=[jax.ShapeDtypeStruct((chunks, plan...  13.3 us
    pallas_call x1, Pallas kernels, local(): pl.pallas_call(functools.partial(correlate_kernel, last=last), grid=(CH /...  12.6 us

profile of v1, /device:TPU:1, one launch (start us, length us, event | category | flops | bytes accessed | tf_op | source)
XLA Modules:
  0.0 104.2 jit_solution(14723917797303399451)
XLA Ops:
  0.0 13.3 %plan.1 = (bf16[8,4,128,256]{3,2,1,0:T(8,128)(2,1)S(1)}, s32[1,2048]{1,0:T(1,128)S(1)}, s32[1]{0:T(128)}) custom-call(bf16[256,2048]{1,0:T(8,128)(2,1)} %records_ref.1, s32[1,256]{1,0:T(1,128)} %bitcast.10, s32[1,256]{1,0:T(1,128)} %bitcast.11, s32[1,256]{1,0:T(1,128)} %bitcast.12), custom_call_target="tpu_custom_call" | custom-call | tf_op jit(solution)/shard_map/plan/pallas_call | solution.py:410
  13.9 77.8 %conditional.1 = (bf16[256,1024]{1,0:T(8,128)(2,1)S(1)}, f32[8,16,1024]{2,1,0:T(8,128)S(1)}) conditional(s32[]{:T(128)} %bitcast.6, (bf16[8,4,128,256]{3,2,1,0:T(8,128)(2,1)S(1)}, s32[1,2048]{1,0:T(1,128)S(1)}, s32[2]{0:T(128)}, bf16[2048,512]{1,0:T(8,128)(2,1)}) %tuple.20, (bf16[8,4,128,256]{3,2,1,0:T(8,128)(2,1)S(1)}, ...), branch_computations={%region_0.0_spmd, %region_1.0_spmd, %region_2.0_spmd} | conditional | bytes 16 | solution.py:477
  13.9 77.5 %deliver1.1 = (f32[128,1024]{1,0:T(8,128)S(1)}, bf16[256,1024]{1,0:T(8,128)(2,1)S(1)}) custom-call(bf16[8,4,128,256]{3,2,1,0:T(8,128)(2,1)S(1)} %get-tuple-element.36.outgoing_ref, s32[1,2048]{1,0:T(1,128)S(1)} %get-tuple-element.37.goal_ref, s32[2]{0:T(128)} %get-tuple-element.38.masks_ref, bf16[2048,512]{1,0:T(8,128)(2,1)} %get-tuple-element.39.table_hbm), custom_call_target="tpu_custom_call" | custom-call | tf_op jit(solution)/shard_map/cond/branch_0_fun/deliver1/pallas_call | solution.py:439
  91.7 12.6 %correlate.1 = bf16[2,128,128,128]{3,2,1,0:T(8,128)(2,1)} custom-call(s32[2]{0:T(128)} %masks_ref.1, f32[8,16,1024]{2,1,0:T(8,128)S(1)} %get-tuple-element.62.own_ref, bf16[256,1024]{1,0:T(8,128)(2,1)S(1)} %get-tuple-element.63.other_ref, bf16[128,512]{1,0:T(8,128)(2,1)} %constant.11.clone.table_ref), custom_call_target="tpu_custom_call" | custom-call | tf_op jit(solution)/shard_map/correlate/pallas_call | solution.py:481

commit v2 on v1

--- a/solution.py
+++ b/solution.py
@@ -16,6 +16,7 @@
 GROUP = 4
 CHUNK = 256
 PIECES = 4
+FLIGHT = 2
 GAP = 64.0
 LEVELS = ((96, 96, 96, 80, 64, 64, 48, 32), (112, 112, 112, 96, 80, 64, 48, 32))
 VMEM = pl.BlockSpec(memory_space=pltpu.VMEM)
@@ -71,6 +72,7 @@
     held = records_ref.shape[0]
     me, part = lax.axis_index("blk"), lax.axis_index("groups")
     parts = levels.shape[0]
+    shift = most.bit_length() - 1
     plane = lax.div(me, GROUP)
 
     barrier = pltpu.get_barrier_semaphore()
@@ -78,10 +80,13 @@
         pl.semaphore_signal(
             barrier, inc=1, device_id={"blk": met_at(me, distance, owners)}, device_id_type=MESH
         )
-    for distance in range(1, parts):
-        pl.semaphore_signal(
-            barrier, inc=1, device_id={"groups": lax.rem(part + distance, parts)}, device_id_type=MESH
-        )
+    abroad = [
+        (turn, distance, {"groups": lax.rem(part + turn, parts), "blk": met_at(me, distance, owners)})
+        for turn in range(1, parts)
+        for distance in range(owners)
+    ]
+    for _, _, other in abroad:
+        pl.semaphore_signal(barrier, inc=1, device_id=other, device_id_type=MESH)
 
     dest, slot, valid = dest_ref[...], slot_ref[...], valid_ref[...]
     group, within = lax.div(dest, GROUP), lax.rem(dest, GROUP)
@@ -98,22 +103,7 @@
         for c in range(chunks):
             limit = jnp.where(reach == c, rows[c], limit)
         level = level + jnp.max((rank >= limit).astype(jnp.float32), axis=1, keepdims=True)
-    levels[0] = level[:, :128]
-
-    pl.semaphore_wait(barrier, owners - 1 + parts - 1)
-    sideways = []
-    for distance in range(1, parts):
-        sideways.append(
-            pltpu.make_async_remote_copy(
-                src_ref=levels.at[0],
-                dst_ref=levels.at[distance],
-                send_sem=level_sems.at[0, distance],
-                recv_sem=level_sems.at[1, distance],
-                device_id={"groups": lax.rem(part + distance, parts)},
-                device_id_type=MESH,
-            )
-        )
-        sideways[-1].start()
+    levels[0, 0] = level[:, :128]
 
     lines = max(8, planes)
     named = lax.broadcasted_iota(jnp.int32, (lines, held), 0) == group
@@ -129,15 +119,22 @@
     code = spread(within + 1) * 256.0 + spread(slot)
     for p in range(planes):
         outbox[p, 0:1, :] = code[p : p + 1]
-
-    for copy in sideways:
-        copy.wait()
-    level = levels[0]
-    for distance in range(1, parts):
-        level = jnp.maximum(level, levels[distance])
-    for p in range(planes):
-        outbox[p, 1:2, :] = level
+        outbox[p, 1:2, :] = level[:, :128]
+
+    pl.semaphore_wait(barrier, owners * parts - 1)
     copies = []
+    for turn, distance, other in abroad:
+        copies.append(
+            pltpu.make_async_remote_copy(
+                src_ref=levels.at[0, 0],
+                dst_ref=levels.at[turn, distance],
+                send_sem=level_sems.at[0, turn, distance],
+                recv_sem=level_sems.at[1, turn, distance],
+                device_id=other,
+                device_id_type=MESH,
+            )
+        )
+        copies[-1].start()
     for distance in range(owners - 1, 0, -1):
         other = met_at(me, distance, owners)
         copies.append(
@@ -164,25 +161,28 @@
         packed = jnp.dot(place, data, preferred_element_type=jnp.float32)
         outgoing_ref[c] = packed.astype(jnp.bfloat16).reshape(planes, most, wide)
 
+    kept = owners * most
+    at = lax.broadcasted_iota(jnp.int32, (128, kept), 1)
+    sown = lax.broadcasted_iota(jnp.int32, (128, kept), 0) == at - (at >> shift << shift)
+    sown = sown.astype(jnp.float32).astype(jnp.bfloat16)
     for copy in copies:
         copy.wait()
     code = inbox[:, 0, :]
-    level_ref[0] = jnp.max(inbox[:, 1, :]).astype(jnp.int32)
-    kept = owners * most
-    at = lax.broadcasted_iota(jnp.int32, (128, kept), 1)
-    sown = lax.broadcasted_iota(jnp.int32, (128, kept), 0) == lax.rem(at, most)
-    sown = sown.astype(jnp.float32).astype(jnp.bfloat16)
+    level = jnp.max(inbox[:, 1, :], axis=0, keepdims=True)
+    for turn, distance, _ in abroad:
+        level = jnp.maximum(level, levels[turn, distance])
+    level_ref[0] = jnp.max(level).astype(jnp.int32)
     owner = (code * (1.0 / 256.0)).astype(jnp.int32).astype(jnp.float32)
     slots = code - owner * 256.0
     at = lax.broadcasted_iota(jnp.int32, (owners, kept), 1)
-    mine = lax.broadcasted_iota(jnp.int32, (owners, kept), 0) == lax.div(at, most)
+    mine = lax.broadcasted_iota(jnp.int32, (owners, kept), 0) == at >> shift
 
     def line_up(values):
         values = jnp.dot(values.astype(jnp.bfloat16), sown, preferred_element_type=jnp.float32)
         return jnp.sum(jnp.where(mine, values, 0.0), axis=0, keepdims=True).astype(jnp.int32)
 
     slots = line_up(slots)
-    goal = lax.rem(slots, W) * CH + lax.div(slots, W)
+    goal = (slots & (W - 1)) * CH + (slots >> (W.bit_length() - 1))
     goal_ref[...] = jnp.where(line_up(owner) == lax.rem(me, GROUP) + 1, goal, -1)
 
 
@@ -247,15 +247,16 @@
         )
         local[c].start()
 
-    def forward(c, step, part):
-        low, count = (0, 1) if part == 0 else (1 << (part - 1), 1 << (part - 1))
+    def forward(c, step, spot, d):
+        at = lax.div(met_at(me, GROUP * d, owners), GROUP)
         rows = pl.ds(0, caps[c])
-        gathers[c, step, part] = send(
+        target = spot + (1 << step)
+        gathers[c, target, d] = send(
             1 << steps[step],
-            arrived.at[c, pl.ds(low, count), :, rows],
-            arrived.at[c, pl.ds(low + (1 << step), count), :, rows],
-            gather_send.at[c, step, part],
-            gather_recv.at[c, step, part],
+            arrived.at[c, spot, at, rows],
+            arrived.at[c, target, at, rows],
+            gather_send.at[c, target, d],
+            gather_recv.at[c, target, d],
         )
 
     goal = goal_ref[...]
@@ -288,24 +289,27 @@
         begin(c)
     depth = len(steps)
     for turn in range(chunks + depth + 1):
-        for stage in range(depth + 1, -1, -1):
+        for stage in range(depth + 2):
             c = turn - stage
             if not 0 <= c < chunks:
                 continue
             if stage == 0:
-                for d in range(planes - 1, 0, -1):
-                    sent[c, d].wait_recv()
-                local[c].wait()
+                for d in range(planes):
+                    if d == 0:
+                        local[c].wait()
+                    else:
+                        sent[c, d].wait_recv()
+                    for step in range(depth):
+                        forward(c, step, 0, d)
                 if c + ahead < chunks:
                     begin(c + ahead)
-                for step in range(depth):
-                    forward(c, step, 0)
             elif stage <= depth:
-                for part in range(stage):
-                    gathers[c, stage - 1, part].wait_recv()
-                for step in range(stage, depth):
-                    forward(c, step, stage)
-            if stage == depth:
+                for spot in range(1 << (stage - 1), 1 << stage):
+                    for d in range(planes):
+                        gathers[c, spot, d].wait_recv()
+                        for step in range(stage, depth):
+                            forward(c, step, spot, d)
+            else:
                 if c == 0:
                     fetch.wait()
                 compute(c)
@@ -321,6 +325,11 @@
 
     factor = lax.rsqrt(jnp.sum(energy[...], axis=1, keepdims=True) * (1.0 / nfft) + 1e-06)
     far = []
+
+    def far_copy(q):
+        rows = pl.ds(q * size, size)
+        far.append(send(last, tile.at[rows], met_ref.at[rows], far_send.at[q], far_recv.at[q]))
+
     for q in range(PIECES):
         rows = slice(q * size, (q + 1) * size)
         for w in range(W):
@@ -337,18 +346,20 @@
             tile[rows, base + F : base + 2 * F] = imag_part
             own_ref[rows, base : base + F] = real_part.astype(jnp.float32)
             own_ref[rows, base + F : base + 2 * F] = imag_part.astype(jnp.float32)
-        rows = pl.ds(q * size, size)
-        far.append(send(last, tile.at[rows], met_ref.at[rows], far_send.at[q], far_recv.at[q]))
+        if q < FLIGHT:
+            far_copy(q)
 
     hops = {}
     for turn in range(PIECES + len(bits)):
-        for stage in range(len(bits), -1, -1):
+        for stage in range(len(bits) + 1):
             q = turn - stage
             if not 0 <= q < PIECES:
                 continue
             rows = slice(q * size, (q + 1) * size)
             if stage == 0:
                 far[q].wait_recv()
+                if q + FLIGHT < PIECES:
+                    far_copy(q + FLIGHT)
                 value = choose(use_far, met_ref[rows], tile[rows])
             else:
                 hops[stage - 1, q].wait_recv()
@@ -419,10 +430,10 @@
         scratch_shapes=[
             pltpu.VMEM((planes, 2, 128), jnp.float32),
             pltpu.VMEM((owners, 2, 128), jnp.float32),
-            pltpu.VMEM((parts, 1, 128), jnp.float32),
+            pltpu.VMEM((parts, owners, 1, 128), jnp.float32),
             pltpu.SemaphoreType.DMA((owners,)),
             pltpu.SemaphoreType.DMA((owners,)),
-            pltpu.SemaphoreType.DMA((2, parts)),
+            pltpu.SemaphoreType.DMA((2, parts, owners)),
         ],
         compiler_params=pltpu.CompilerParams(
             vmem_limit_bytes=limit, collective_id=0, has_side_effects=True
@@ -455,8 +466,8 @@
                     pltpu.VMEM((hops, CH, width), jnp.bfloat16),
                     pltpu.SemaphoreType.DMA((chunks, planes)),
                     pltpu.SemaphoreType.DMA((chunks, planes)),
-                    pltpu.SemaphoreType.DMA((chunks, depth, depth)),
-                    pltpu.SemaphoreType.DMA((chunks, depth, depth)),
+                    pltpu.SemaphoreType.DMA((chunks, GROUP, planes)),
+                    pltpu.SemaphoreType.DMA((chunks, GROUP, planes)),
                     pltpu.SemaphoreType.DMA((chunks,)),
                     pltpu.SemaphoreType.DMA,
                     pltpu.SemaphoreType.DMA((PIECES,)),

time: 104 us -> 92.9 us (0.89)
  Pallas kernels: 103 us -> 91.9 us
    pallas_call x1, Pallas kernels: 77.5 us -> 67.4 us  [call(): pl.pallas_call(functools.partial(deliver_kernel, caps), out_shape=[jax.Sh...]
    pallas_call x1, Pallas kernels: 13.3 us -> 11.9 us  [local(): pl.pallas_call(plan_kernel, out_shape=[jax.ShapeDtypeStruct((chunks, plan...]
where the time goes in v2:
time: 92.9 us; the launch traced here: 92.7 us
  Pallas kernels  91.9 us (99%)
    pallas_call x1, Pallas kernels, call(): pl.pallas_call(functools.partial(deliver_kernel, caps), out_shape=[jax.Sh...  67.4 us
    pallas_call x1, Pallas kernels, local(): pl.pallas_call(functools.partial(correlate_kernel, last=last), grid=(CH /...  12.6 us
    pallas_call x1, Pallas kernels, local(): pl.pallas_call(plan_kernel, out_shape=[jax.ShapeDtypeStruct((chunks, plan...  11.9 us

profile of v2, /device:TPU:1, one launch (start us, length us, event | category | flops | bytes accessed | tf_op | source)
XLA Modules:
  0.0 92.7 jit_solution(5049151650202020680)
XLA Ops:
  0.0 11.9 %plan.1 = (bf16[8,4,128,256]{3,2,1,0:T(8,128)(2,1)S(1)}, s32[1,2048]{1,0:T(1,128)S(1)}, s32[1]{0:T(128)}) custom-call(bf16[256,2048]{1,0:T(8,128)(2,1)} %records_ref.1, s32[1,256]{1,0:T(1,128)} %bitcast.10, s32[1,256]{1,0:T(1,128)} %bitcast.11, s32[1,256]{1,0:T(1,128)} %bitcast.12), custom_call_target="tpu_custom_call" | custom-call | tf_op jit(solution)/shard_map/plan/pallas_call | solution.py:421
  12.5 67.7 %conditional.1 = (bf16[256,1024]{1,0:T(8,128)(2,1)S(1)}, f32[8,16,1024]{2,1,0:T(8,128)S(1)}) conditional(s32[]{:T(128)} %bitcast.6, (bf16[8,4,128,256]{3,2,1,0:T(8,128)(2,1)S(1)}, s32[1,2048]{1,0:T(1,128)S(1)}, s32[2]{0:T(128)}, bf16[2048,512]{1,0:T(8,128)(2,1)}) %tuple.20, (bf16[8,4,128,256]{3,2,1,0:T(8,128)(2,1)S(1)}, ...), branch_computations={%region_0.0_spmd, %region_1.0_spmd, %region_2.0_spmd} | conditional | bytes 16 | solution.py:488
  12.5 67.4 %deliver1.1 = (f32[128,1024]{1,0:T(8,128)S(1)}, bf16[256,1024]{1,0:T(8,128)(2,1)S(1)}) custom-call(bf16[8,4,128,256]{3,2,1,0:T(8,128)(2,1)S(1)} %get-tuple-element.36.outgoing_ref, s32[1,2048]{1,0:T(1,128)S(1)} %get-tuple-element.37.goal_ref, s32[2]{0:T(128)} %get-tuple-element.38.masks_ref, bf16[2048,512]{1,0:T(8,128)(2,1)} %get-tuple-element.39.table_hbm), custom_call_target="tpu_custom_call" | custom-call | tf_op jit(solution)/shard_map/cond/branch_0_fun/deliver1/pallas_call | solution.py:450
  80.2 12.6 %correlate.1 = bf16[2,128,128,128]{3,2,1,0:T(8,128)(2,1)} custom-call(s32[2]{0:T(128)} %masks_ref.1, f32[8,16,1024]{2,1,0:T(8,128)S(1)} %get-tuple-element.62.own_ref, bf16[256,1024]{1,0:T(8,128)(2,1)S(1)} %get-tuple-element.63.other_ref, bf16[128,512]{1,0:T(8,128)(2,1)} %constant.11.clone.table_ref), custom_call_target="tpu_custom_call" | custom-call | tf_op jit(solution)/shard_map/correlate/pallas_call | solution.py:492
